TPU v7x, 32 devices: a whole 2x2x4 slice. The times are simulated.
32 devices in a mesh: panel: 4 (over x, core), front: 8 (over z, y).
Axes of the slice: x: 2, y: 2, z: 4, core: 2. Of those that a mesh axis runs over, the one named last changes fastest.
Arguments:
- rhs: float32 [4, 64, 64, 2, 128], P('panel', None, 'front'), may hold values from -6 to 6
- fronts: bfloat16 [4, 2, 8192, 8192], P('panel', None, 'front'), may hold values from -0.046875 to 0.046875
- wave_sq: float32 [4, 64, 128], P('panel', 'front'), may hold values from 0.5 to 2
- pml_width: int32 [4], P('panel'), may hold values from 1 to 16
Outputs:
- sweep_field: float32 [4, 64, 64, 2, 128], P('panel', None, 'front')
- residual: float32 [4, 64, 64, 2, 128], P('panel', None, 'front')
All inputs are finite; a program needn't handle non-finite values.
Results may differ from a plain program's by a relative error of at most 0.013.
Values may be sent and summed in bfloat16 or wider, within the bound.
No kernel may reach another device: no remote copies, remote signals or barrier semaphores. Data moves between devices by JAX's collectives and lax.ppermute only.
A program may use at most 64 MiB of HBM per device.

v0:
```python
import jax
import jax.numpy as jnp
from jax import lax
from jax.sharding import PartitionSpec as P


def from_behind(shard, axis, by):
    devices = lax.axis_size(axis)
    pairs = [(i, i + by) for i in range(devices) if 0 <= i + by < devices]
    return lax.ppermute(shard, axis, pairs)


def padded_2(cells, sides, width):
    for axis, dim in sides:
        count = lax.axis_size(axis)
        ends = count - 1
        head = lax.slice_in_dim(cells, 0, width, axis=dim)
        tail = lax.slice_in_dim(cells, cells.shape[dim] - width, cells.shape[dim], axis=dim)
        cells = jnp.concatenate(
            [
                lax.ppermute(tail, axis, [(i, (i + 1) % count) for i in range(ends)]),
                cells,
                lax.ppermute(head, axis, [((i + 1) % count, i) for i in range(ends)]),
            ],
            axis=dim,
        )
    return cells


def local(rhs, fronts, wave_sq, pml_width):
    group_panels, rhs_count, row_count, components, columns = rhs.shape
    panel_count = lax.axis_size("panel")
    group_index = lax.axis_index("panel")
    block_count = 1
    block_size = rhs_count // block_count

    def apply_front(combined, local_panel):
        front_re = fronts[local_panel, 0]
        front_im = fronts[local_panel, 1]
        vector_piece = lax.all_gather(combined, "front", axis=1, tiled=True)
        piece_rows = vector_piece.shape[1]
        width = piece_rows * columns
        part_re = vector_piece[:, :, 0].reshape(block_size, width)
        part_im = vector_piece[:, :, 1].reshape(block_size, width)
        dims = (((1,), (1,)), ((), ()))
        new_re = lax.dot_general(
            part_re, front_re, dims, preferred_element_type=jnp.float32
        ) - lax.dot_general(part_im, front_im, dims, preferred_element_type=jnp.float32)
        new_im = lax.dot_general(
            part_re, front_im, dims, preferred_element_type=jnp.float32
        ) + lax.dot_general(part_im, front_re, dims, preferred_element_type=jnp.float32)
        return jnp.stack(
            [
                new_re.reshape(block_size, row_count, columns),
                new_im.reshape(block_size, row_count, columns),
            ],
            axis=2,
        )

    def one_section(section_num, carry):
        solved_all, incoming = carry
        block_num = section_num - group_index
        active = (block_num >= 0) & (block_num < block_count)
        previous = incoming
        rhs_block = rhs[0]
        combined = (rhs_block + previous).astype(jnp.bfloat16)
        solved = apply_front(combined, 0)
        earlier = solved_all
        solved_all = jnp.where(active, solved[None], earlier)
        incoming = from_behind(solved, "panel", 1)
        return (solved_all, incoming)

    start_all = jnp.zeros(rhs.shape, jnp.float32)
    start_in = jnp.zeros((block_size, row_count, components, columns), jnp.float32)
    sweep_field, _ = lax.fori_loop(
        0, panel_count + block_count - 1, one_section, (start_all, start_in)
    )
    padded = padded_2(sweep_field.astype(jnp.bfloat16), (("panel", 0), ("front", 2)), 1).astype(
        sweep_field.dtype
    )
    beside = padded[2:, :, 1:-1] + padded[:-2, :, 1:-1]
    beside = beside + padded[1:-1, :, 2:] + padded[1:-1, :, :-2]
    side_pad = jnp.pad(sweep_field, ((0, 0), (0, 0), (0, 0), (0, 0), (1, 1)))
    beside = beside + side_pad[..., 2:] + side_pad[..., :-2]
    plane_rows = lax.axis_index("front") * row_count + jnp.arange(row_count, dtype=jnp.int32)
    row_pos = plane_rows.astype(jnp.float32)[None, :]
    total_rows = row_count * lax.axis_size("front")
    thick = pml_width.astype(jnp.float32)[:, None]
    absorb = (
        2.0
        * (jnp.maximum(0.0, thick - row_pos) + jnp.maximum(0.0, row_pos - (total_rows - 1 - thick)))
        / thick
    )
    absorb_b = absorb[:, None, :, None]
    diagonal_term = (6.0 - wave_sq)[:, None, :, :]
    real_part = sweep_field[:, :, :, 0]
    imag_part = sweep_field[:, :, :, 1]
    apply_re = diagonal_term * real_part - absorb_b * imag_part - beside[:, :, :, 0]
    apply_im = diagonal_term * imag_part + absorb_b * real_part - beside[:, :, :, 1]
    residual = rhs - jnp.stack([apply_re, apply_im], axis=3)
    return (sweep_field, residual)


def solution(mesh):
    return jax.shard_map(
        local,
        mesh=mesh,
        in_specs=(
            P("panel", None, "front", None, None),
            P("panel", None, "front", None),
            P("panel", "front", None),
            P("panel"),
        ),
        out_specs=(P("panel", None, "front", None, None), P("panel", None, "front", None, None)),
        check_vma=False,
    )
```

profile of v0, /device:TPU:10, one launch (start us, length us, event | category | flops | bytes accessed | tf_op | source)
XLA Modules:
  0.0 458.6 jit_solution(15256250120979236043)
XLA Ops:
  9.1 416.1 %while.16 = (s32[]{:T(128)}, f32[1,64,8,2,128]{4,2,1,3,0:T(8,128)S(1)}, f32[64,8,2,128]{3,1,0,2:T(8,128)}, s32[]{:T(128)}, f32[1,64,8,2,128]{4,2,1,3,0:T(8,128)S...) while((s32[]{:T(128)}, f32[1,64,8,2,128]{4,2,1,3,0:T(8,128)S(1)}, ...), condition=%wide.region_1.2_spmd.clone, body=%wide.region_0.1_spmd.clone.sunk | while | flops 4295622656 | bytes 91226304 | solution.py:75
  11.0 52.0 %all-gather.2.cloned.1.call-done = bf16[64,64,2,128]{3,1,0,2:T(8,128)(2,1)} async-done(((bf16[64,8,2,128]{3,1,0,2:T(8,128)(2,1)}), bf16[64,64,2,128]{3,1,0,2:T(8,128)(2,1)}) %all-gather.2.cloned.1.call-update) | async-done | bytes 2097168 | tf_op jit(solution)/shard_map/while/body/eval_jaxpr/all_gather | solution.py:40
  64.6 10.0 %fusion.63 = f32[64,1024]{1,0:T(8,128)} fusion(bf16[1,2,1024,8192]{3,2,1,0:T(8,128)(2,1)} %get-tuple-element.223, bf16[8,8,64,128]{3,2,1,0:T(8,128)(2,1)S(1)} %bitcast.88), kind=kOutput, calls=%fused_computation.clone.1 | convolution fusion | flops 1073741824 | bytes 18087936 | tf_op jit(solution)/shard_map/while/body/eval_jaxpr/dot_general | solution.py:49
  74.6 10.0 %fusion.61 = f32[64,1024]{1,0:T(8,128)} fusion(bf16[1,2,1024,8192]{3,2,1,0:T(8,128)(2,1)} %get-tuple-element.223, bf16[8,8,64,128]{3,2,1,0:T(8,128)(2,1)S(1)} %bitcast.90), kind=kOutput, calls=%fused_computation.2.clone.1 | convolution fusion | flops 1073741824 | bytes 18087936 | tf_op jit(solution)/shard_map/while/body/eval_jaxpr/dot_general | solution.py:48
  84.6 9.3 %fusion.64 = f32[8,8,8,128]{3,1,2,0:T(8,128)S(1)} fusion(f32[64,1024]{1,0:T(8,128)} %fusion.63, bf16[1,2,1024,8192]{3,2,1,0:T(8,128)(2,1)} %get-tuple-element.223, bf16[8,8,64,128]{3,2,1,0:T(8,128)(2,1)S(1)} %bitcast.91), kind=kOutput, calls=%fused_computation.15.clone.1 | convolution fusion | flops 1073807360 | bytes 18350080 | tf_op jit(solution)/shard_map/while/body/eval_jaxpr/dot_general | solution.py:51
  94.0 9.3 %fusion.62 = f32[8,8,8,128]{3,1,2,0:T(8,128)S(1)} fusion(f32[64,1024]{1,0:T(8,128)} %fusion.61, bf16[1,2,1024,8192]{3,2,1,0:T(8,128)(2,1)} %get-tuple-element.223, bf16[8,8,64,128]{3,2,1,0:T(8,128)(2,1)S(1)} %bitcast.89), kind=kOutput, calls=%fused_computation.13.clone.1 | convolution fusion | flops 1073807360 | bytes 18350080 | tf_op jit(solution)/shard_map/while/body/eval_jaxpr/dot_general | solution.py:46
  103.4 1.9 collective-permute-start
  105.5 8.5 %collective-permute-done = f32[64,8,2,128]{3,1,0,2:T(8,128)} collective-permute-done((f32[64,8,2,128]{3,1,0,2:T(8,128)S(1)}, f32[64,8,2,128]{3,1,0,2:T(8,128)}, u32[]{:S(2)}, u32[]{:S(2)}) %collective-permute-start) | collective-permute-done | bytes 524320 | tf_op jit(solution)/shard_map/while/body/eval_jaxpr/ppermute | solution.py:10
  115.9 50.9 %all-gather.2.cloned.1.call-done = bf16[64,64,2,128]{3,1,0,2:T(8,128)(2,1)} async-done(((bf16[64,8,2,128]{3,1,0,2:T(8,128)(2,1)}), bf16[64,64,2,128]{3,1,0,2:T(8,128)(2,1)}) %all-gather.2.cloned.1.call-update) | async-done | bytes 2097168 | tf_op jit(solution)/shard_map/while/body/eval_jaxpr/all_gather | solution.py:40
  168.5 10.0 %fusion.63 = f32[64,1024]{1,0:T(8,128)} fusion(bf16[1,2,1024,8192]{3,2,1,0:T(8,128)(2,1)} %get-tuple-element.223, bf16[8,8,64,128]{3,2,1,0:T(8,128)(2,1)S(1)} %bitcast.88), kind=kOutput, calls=%fused_computation.clone.1 | convolution fusion | flops 1073741824 | bytes 18087936 | tf_op jit(solution)/shard_map/while/body/eval_jaxpr/dot_general | solution.py:49
  178.5 10.0 %fusion.61 = f32[64,1024]{1,0:T(8,128)} fusion(bf16[1,2,1024,8192]{3,2,1,0:T(8,128)(2,1)} %get-tuple-element.223, bf16[8,8,64,128]{3,2,1,0:T(8,128)(2,1)S(1)} %bitcast.90), kind=kOutput, calls=%fused_computation.2.clone.1 | convolution fusion | flops 1073741824 | bytes 18087936 | tf_op jit(solution)/shard_map/while/body/eval_jaxpr/dot_general | solution.py:48
  188.4 9.3 %fusion.64 = f32[8,8,8,128]{3,1,2,0:T(8,128)S(1)} fusion(f32[64,1024]{1,0:T(8,128)} %fusion.63, bf16[1,2,1024,8192]{3,2,1,0:T(8,128)(2,1)} %get-tuple-element.223, bf16[8,8,64,128]{3,2,1,0:T(8,128)(2,1)S(1)} %bitcast.91), kind=kOutput, calls=%fused_computation.15.clone.1 | convolution fusion | flops 1073807360 | bytes 18350080 | tf_op jit(solution)/shard_map/while/body/eval_jaxpr/dot_general | solution.py:51
  197.8 9.3 %fusion.62 = f32[8,8,8,128]{3,1,2,0:T(8,128)S(1)} fusion(f32[64,1024]{1,0:T(8,128)} %fusion.61, bf16[1,2,1024,8192]{3,2,1,0:T(8,128)(2,1)} %get-tuple-element.223, bf16[8,8,64,128]{3,2,1,0:T(8,128)(2,1)S(1)} %bitcast.89), kind=kOutput, calls=%fused_computation.13.clone.1 | convolution fusion | flops 1073807360 | bytes 18350080 | tf_op jit(solution)/shard_map/while/body/eval_jaxpr/dot_general | solution.py:46
  207.3 1.9 collective-permute-start
  209.4 8.5 %collective-permute-done = f32[64,8,2,128]{3,1,0,2:T(8,128)} collective-permute-done((f32[64,8,2,128]{3,1,0,2:T(8,128)S(1)}, f32[64,8,2,128]{3,1,0,2:T(8,128)}, u32[]{:S(2)}, u32[]{:S(2)}) %collective-permute-start) | collective-permute-done | bytes 524320 | tf_op jit(solution)/shard_map/while/body/eval_jaxpr/ppermute | solution.py:10
  219.7 50.9 %all-gather.2.cloned.1.call-done = bf16[64,64,2,128]{3,1,0,2:T(8,128)(2,1)} async-done(((bf16[64,8,2,128]{3,1,0,2:T(8,128)(2,1)}), bf16[64,64,2,128]{3,1,0,2:T(8,128)(2,1)}) %all-gather.2.cloned.1.call-update) | async-done | bytes 2097168 | tf_op jit(solution)/shard_map/while/body/eval_jaxpr/all_gather | solution.py:40
  272.3 10.0 %fusion.63 = f32[64,1024]{1,0:T(8,128)} fusion(bf16[1,2,1024,8192]{3,2,1,0:T(8,128)(2,1)} %get-tuple-element.223, bf16[8,8,64,128]{3,2,1,0:T(8,128)(2,1)S(1)} %bitcast.88), kind=kOutput, calls=%fused_computation.clone.1 | convolution fusion | flops 1073741824 | bytes 18087936 | tf_op jit(solution)/shard_map/while/body/eval_jaxpr/dot_general | solution.py:49
  282.3 10.0 %fusion.61 = f32[64,1024]{1,0:T(8,128)} fusion(bf16[1,2,1024,8192]{3,2,1,0:T(8,128)(2,1)} %get-tuple-element.223, bf16[8,8,64,128]{3,2,1,0:T(8,128)(2,1)S(1)} %bitcast.90), kind=kOutput, calls=%fused_computation.2.clone.1 | convolution fusion | flops 1073741824 | bytes 18087936 | tf_op jit(solution)/shard_map/while/body/eval_jaxpr/dot_general | solution.py:48
  292.3 9.3 %fusion.64 = f32[8,8,8,128]{3,1,2,0:T(8,128)S(1)} fusion(f32[64,1024]{1,0:T(8,128)} %fusion.63, bf16[1,2,1024,8192]{3,2,1,0:T(8,128)(2,1)} %get-tuple-element.223, bf16[8,8,64,128]{3,2,1,0:T(8,128)(2,1)S(1)} %bitcast.91), kind=kOutput, calls=%fused_computation.15.clone.1 | convolution fusion | flops 1073807360 | bytes 18350080 | tf_op jit(solution)/shard_map/while/body/eval_jaxpr/dot_general | solution.py:51
  301.6 9.3 %fusion.62 = f32[8,8,8,128]{3,1,2,0:T(8,128)S(1)} fusion(f32[64,1024]{1,0:T(8,128)} %fusion.61, bf16[1,2,1024,8192]{3,2,1,0:T(8,128)(2,1)} %get-tuple-element.223, bf16[8,8,64,128]{3,2,1,0:T(8,128)(2,1)S(1)} %bitcast.89), kind=kOutput, calls=%fused_computation.13.clone.1 | convolution fusion | flops 1073807360 | bytes 18350080 | tf_op jit(solution)/shard_map/while/body/eval_jaxpr/dot_general | solution.py:46
  313.2 8.5 %collective-permute-done = f32[64,8,2,128]{3,1,0,2:T(8,128)} collective-permute-done((f32[64,8,2,128]{3,1,0,2:T(8,128)S(1)}, f32[64,8,2,128]{3,1,0,2:T(8,128)}, u32[]{:S(2)}, u32[]{:S(2)}) %collective-permute-start) | collective-permute-done | bytes 524320 | tf_op jit(solution)/shard_map/while/body/eval_jaxpr/ppermute | solution.py:10
  323.6 50.5 %all-gather.2.cloned.1.call-done = bf16[64,64,2,128]{3,1,0,2:T(8,128)(2,1)} async-done(((bf16[64,8,2,128]{3,1,0,2:T(8,128)(2,1)}), bf16[64,64,2,128]{3,1,0,2:T(8,128)(2,1)}) %all-gather.2.cloned.1.call-update) | async-done | bytes 2097168 | tf_op jit(solution)/shard_map/while/body/eval_jaxpr/all_gather | solution.py:40
  375.8 10.0 %fusion.63 = f32[64,1024]{1,0:T(8,128)} fusion(bf16[1,2,1024,8192]{3,2,1,0:T(8,128)(2,1)} %get-tuple-element.223, bf16[8,8,64,128]{3,2,1,0:T(8,128)(2,1)S(1)} %bitcast.88), kind=kOutput, calls=%fused_computation.clone.1 | convolution fusion | flops 1073741824 | bytes 18087936 | tf_op jit(solution)/shard_map/while/body/eval_jaxpr/dot_general | solution.py:49
  385.8 10.0 %fusion.61 = f32[64,1024]{1,0:T(8,128)} fusion(bf16[1,2,1024,8192]{3,2,1,0:T(8,128)(2,1)} %get-tuple-element.223, bf16[8,8,64,128]{3,2,1,0:T(8,128)(2,1)S(1)} %bitcast.90), kind=kOutput, calls=%fused_computation.2.clone.1 | convolution fusion | flops 1073741824 | bytes 18087936 | tf_op jit(solution)/shard_map/while/body/eval_jaxpr/dot_general | solution.py:48
  395.8 9.3 %fusion.64 = f32[8,8,8,128]{3,1,2,0:T(8,128)S(1)} fusion(f32[64,1024]{1,0:T(8,128)} %fusion.63, bf16[1,2,1024,8192]{3,2,1,0:T(8,128)(2,1)} %get-tuple-element.223, bf16[8,8,64,128]{3,2,1,0:T(8,128)(2,1)S(1)} %bitcast.91), kind=kOutput, calls=%fused_computation.15.clone.1 | convolution fusion | flops 1073807360 | bytes 18350080 | tf_op jit(solution)/shard_map/while/body/eval_jaxpr/dot_general | solution.py:51
  405.1 9.3 %fusion.62 = f32[8,8,8,128]{3,1,2,0:T(8,128)S(1)} fusion(f32[64,1024]{1,0:T(8,128)} %fusion.61, bf16[1,2,1024,8192]{3,2,1,0:T(8,128)(2,1)} %get-tuple-element.223, bf16[8,8,64,128]{3,2,1,0:T(8,128)(2,1)S(1)} %bitcast.89), kind=kOutput, calls=%fused_computation.13.clone.1 | convolution fusion | flops 1073807360 | bytes 18350080 | tf_op jit(solution)/shard_map/while/body/eval_jaxpr/dot_general | solution.py:46
  416.7 8.5 %collective-permute-done = f32[64,8,2,128]{3,1,0,2:T(8,128)} collective-permute-done((f32[64,8,2,128]{3,1,0,2:T(8,128)S(1)}, f32[64,8,2,128]{3,1,0,2:T(8,128)}, u32[]{:S(2)}, u32[]{:S(2)}) %collective-permute-start) | collective-permute-done | bytes 524320 | tf_op jit(solution)/shard_map/while/body/eval_jaxpr/ppermute | solution.py:10
  427.7 3.6 collective-permute-start.2
  435.5 2.6 collective-permute-start.3
  438.1 4.7 %collective-permute-start.4 = (bf16[3,64,1,2,128]{4,3,2,1,0:T(2,128)(2,1)S(1)}, bf16[3,64,1,2,128]{4,3,2,1,0:T(2,128)(2,1)S(1)}, u32[]{:S(2)}, u32[]{:S(2)}) collective-permute-start(bf16[3,64,1,2,128]{4,3,2,1,0:T(2,128)(2,1)S(1)} %get-tuple-element.160), channel_id=1, source_target_pairs={{1,0},{2,1},{3,2},{4,3},{5,4},{6,5},{7,6},{9,8},{10,9},{11,10},{12... | collective-permute-start | bytes 294920 | tf_op jit(solution)/shard_map/ppermute | solution.py:23
  443.3 2.6 collective-permute-done.4
  449.7 2.4 maximum_subtract_fusion
  (56 shorter events, 31.4 us)
Async XLA Ops:
  9.1 422.9 %copy-start.1 = (f32[1,8,128]{2,1,0:T(8,128)S(1)}, f32[1,8,128]{2,1,0:T(8,128)}, u32[]{:S(2)}) copy-start(f32[1,8,128]{2,1,0:T(8,128)} %param.8) | copy-start | bytes 12292
  9.1 53.8 %all-gather.2.cloned.1.call-start = ((), (), s32[]{:S(2)}) async-start(), calls=%async_computation | async-start | bytes 2359296 | tf_op jit(solution)/shard_map/while/body/eval_jaxpr/all_gather | solution.py:40
  103.4 10.6 %collective-permute-start = (f32[64,8,2,128]{3,1,0,2:T(8,128)S(1)}, f32[64,8,2,128]{3,1,0,2:T(8,128)}, u32[]{:S(2)}, u32[]{:S(2)}) collective-permute-start(f32[64,8,2,128]{3,1,0,2:T(8,128)S(1)} %constant_dynamic-update-slice_fusion.5), channel_id=1, source_target_pairs={{0,8},{8,16},{16,24},{1,9},{9,17},{17,25},{2,10},{10,18},{18,26},{... | collective-permute-start | bytes 1572872 | tf_op jit(solution)/shard_map/while/body/eval_jaxpr/ppermute | solution.py:10
  114.0 52.7 %all-gather.2.cloned.1.call-start = ((), (), s32[]{:S(2)}) async-start(), calls=%async_computation | async-start | bytes 2359296 | tf_op jit(solution)/shard_map/while/body/eval_jaxpr/all_gather | solution.py:40
  207.3 10.6 %collective-permute-start = (f32[64,8,2,128]{3,1,0,2:T(8,128)S(1)}, f32[64,8,2,128]{3,1,0,2:T(8,128)}, u32[]{:S(2)}, u32[]{:S(2)}) collective-permute-start(f32[64,8,2,128]{3,1,0,2:T(8,128)S(1)} %constant_dynamic-update-slice_fusion.5), channel_id=1, source_target_pairs={{0,8},{8,16},{16,24},{1,9},{9,17},{17,25},{2,10},{10,18},{18,26},{... | collective-permute-start | bytes 1572872 | tf_op jit(solution)/shard_map/while/body/eval_jaxpr/ppermute | solution.py:10
  217.9 52.7 %all-gather.2.cloned.1.call-start = ((), (), s32[]{:S(2)}) async-start(), calls=%async_computation | async-start | bytes 2359296 | tf_op jit(solution)/shard_map/while/body/eval_jaxpr/all_gather | solution.py:40
  311.1 10.6 %collective-permute-start = (f32[64,8,2,128]{3,1,0,2:T(8,128)S(1)}, f32[64,8,2,128]{3,1,0,2:T(8,128)}, u32[]{:S(2)}, u32[]{:S(2)}) collective-permute-start(f32[64,8,2,128]{3,1,0,2:T(8,128)S(1)} %constant_dynamic-update-slice_fusion.5), channel_id=1, source_target_pairs={{0,8},{8,16},{16,24},{1,9},{9,17},{17,25},{2,10},{10,18},{18,26},{... | collective-permute-start | bytes 1572872 | tf_op jit(solution)/shard_map/while/body/eval_jaxpr/ppermute | solution.py:10
  321.7 52.4 %all-gather.2.cloned.1.call-start = ((), (), s32[]{:S(2)}) async-start(), calls=%async_computation | async-start | bytes 2359296 | tf_op jit(solution)/shard_map/while/body/eval_jaxpr/all_gather | solution.py:40
  414.6 10.6 %collective-permute-start = (f32[64,8,2,128]{3,1,0,2:T(8,128)S(1)}, f32[64,8,2,128]{3,1,0,2:T(8,128)}, u32[]{:S(2)}, u32[]{:S(2)}) collective-permute-start(f32[64,8,2,128]{3,1,0,2:T(8,128)S(1)} %constant_dynamic-update-slice_fusion.5), channel_id=1, source_target_pairs={{0,8},{8,16},{16,24},{1,9},{9,17},{17,25},{2,10},{10,18},{18,26},{... | collective-permute-start | bytes 1572872 | tf_op jit(solution)/shard_map/while/body/eval_jaxpr/ppermute | solution.py:10
  425.7 26.3 %copy-start = (f32[1,64,8,2,128]{4,3,2,1,0:T(2,128)}, f32[1,64,8,2,128]{4,3,2,1,0:T(2,128)S(1)}, u32[]{:S(2)}) copy-start(f32[1,64,8,2,128]{4,3,2,1,0:T(2,128)S(1)} %get-tuple-element.154) | copy-start | bytes 1572868
  425.8 7.7 %collective-permute-start.1 = (bf16[1,64,8,2,128]{4,3,2,1,0:T(2,128)(2,1)S(1)}, bf16[1,64,8,2,128]{4,3,2,1,0:T(2,128)(2,1)S(1)}, u32[]{:S(2)}, u32[]{:S(2)}) collective-permute-start(bf16[1,64,8,2,128]{4,3,2,1,0:T(2,128)(2,1)S(1)} %get-tuple-element.153), channel_id=1, source_target_pairs={{0,8},{8,16},{16,24},{1,9},{9,17},{17,25},{2,10},{10,18},{18,26},{... | collective-permute-start | bytes 786440 | tf_op jit(solution)/shard_map/ppermute | solution.py:21
  427.7 7.5 %collective-permute-start.2 = (bf16[1,64,8,2,128]{4,3,2,1,0:T(2,128)(2,1)S(1)}, bf16[1,64,8,2,128]{4,3,2,1,0:T(2,128)(2,1)S(1)}, u32[]{:S(2)}, u32[]{:S(2)}) collective-permute-start(bf16[1,64,8,2,128]{4,3,2,1,0:T(2,128)(2,1)S(1)} %get-tuple-element.153), channel_id=1, source_target_pairs={{8,0},{16,8},{24,16},{9,1},{17,9},{25,17},{10,2},{18,10},{26,18},{... | collective-permute-start | bytes 786440 | tf_op jit(solution)/shard_map/ppermute | solution.py:23
  435.5 7.8 %collective-permute-start.3 = (bf16[3,64,1,2,128]{4,3,2,1,0:T(2,128)(2,1)S(1)}, bf16[3,64,1,2,128]{4,3,2,1,0:T(2,128)(2,1)S(1)}, u32[]{:S(2)}, u32[]{:S(2)}) collective-permute-start(bf16[3,64,1,2,128]{4,3,2,1,0:T(2,128)(2,1)S(1)} %get-tuple-element.159), channel_id=1, source_target_pairs={{0,1},{1,2},{2,3},{3,4},{4,5},{5,6},{6,7},{8,9},{9,10},{10,11},{11... | collective-permute-start | bytes 294920 | tf_op jit(solution)/shard_map/ppermute | solution.py:21
  438.1 7.7 %collective-permute-start.4 = (bf16[3,64,1,2,128]{4,3,2,1,0:T(2,128)(2,1)S(1)}, bf16[3,64,1,2,128]{4,3,2,1,0:T(2,128)(2,1)S(1)}, u32[]{:S(2)}, u32[]{:S(2)}) collective-permute-start(bf16[3,64,1,2,128]{4,3,2,1,0:T(2,128)(2,1)S(1)} %get-tuple-element.160), channel_id=1, source_target_pairs={{1,0},{2,1},{3,2},{4,3},{5,4},{6,5},{7,6},{9,8},{10,9},{11,10},{12... | collective-permute-start | bytes 294920 | tf_op jit(solution)/shard_map/ppermute | solution.py:23
Sparse Core Ops, SparseCore 0:
  12.5 50.3 all-gather.1
  117.5 49.2 all-gather.1
  221.3 49.2 all-gather.1
  324.8 49.2 all-gather.1
where the time goes:
time: 462 us; the launch traced here: 459 us
  waiting for transfers between devices  245 us (53%)
  matrix products  154 us (33%)
  starting transfers between devices  20.5 us (4%)
  other arithmetic  15.1 us (3%)
  between operations  14.5 us (3%)
  local copies, waits for them, and re-layouts  9.31 us (2%)
    all_gather x4, waiting for transfers between devices, apply_front(): vector_piece = lax.all_gather(combined, 'front', axis=1, tiled=True)  204 us
    dot_general x4, matrix products, apply_front(): lax.dot_general(part_re, front_im, dims, preferred_element_type=jnp.float32)  39.9 us
    dot_general x4, matrix products, apply_front(): lax.dot_general(part_im, front_im, dims, preferred_element_type=jnp.float32)  39.9 us
    dot_general x4, matrix products, apply_front(): lax.dot_general(part_re, front_re, dims, preferred_element_type=jnp.float32)  37.3 us
    dot_general x4, matrix products, apply_front(): lax.dot_general(part_im, front_re, dims, preferred_element_type=jnp.float32)  37.3 us
    ppermute x4, waiting for transfers between devices, from_behind(): return lax.ppermute(shard, axis, pairs)  34 us
  transfers between devices with their start and end apart: 12, of which 12 were waited for; matrix products, arithmetic and copies ran while one was open for 0% of the time, Pallas kernels for 0%

commit v1 on v0

v1 whole, which is shorter than its diff:
```python
import functools

import jax
import jax.numpy as jnp
from jax import lax
from jax.experimental import pallas as pl
from jax.experimental.pallas import tpu as pltpu
from jax.sharding import PartitionSpec as P


def mul_kernel(first, last, ids_ref, x_ref, c_ref, *refs):
    refs = list(refs)
    acc_in = None if first else refs.pop(0)
    rhs_ref = refs.pop(0) if last else None
    s_ref = refs.pop(0) if last else None
    k = pl.program_id(1)
    count = pl.num_programs(1)

    if last:

        @pl.when(ids_ref[0] == 0)
        def _():
            refs[0][...] = s_ref[...]

    @pl.when(ids_ref[0] == 1)
    def _():
        acc = refs[-1]
        x = x_ref[k]
        re = jnp.dot(c_ref[0, 0], x, preferred_element_type=jnp.float32)
        im = jnp.dot(c_ref[0, 1], x, preferred_element_type=jnp.float32)

        @pl.when(k == 0)
        def _():
            if first:
                acc[0] = re
                acc[1] = im
            else:
                acc[0] = acc_in[0] + re
                acc[1] = acc_in[1] + im

        @pl.when(k > 0)
        def _():
            acc[0] += re
            acc[1] += im

        if last:

            @pl.when(k == count - 1)
            def _():
                half = x.shape[1] // 2
                turn = acc[1]
                s = acc[0] + jnp.concatenate([-turn[:, half:], turn[:, :half]], axis=1)
                refs[0][...] = s
                refs[1][...] = (rhs_ref[...] + s).astype(jnp.bfloat16)


def multiply(ids, x, fronts, acc=None, rhs=None, s=None):
    count, width, lanes = x.shape
    rows = fronts.shape[2]
    tile = min(rows, 512)
    first, last = acc is None, rhs is not None

    def front_block(i, k, ids):
        return (0, 0, i * ids[0], ids[1 + k] * ids[0])

    acc_spec = pl.BlockSpec((2, tile, lanes), lambda i, k, ids: (0, i, 0))
    row_spec = pl.BlockSpec((tile, lanes), lambda i, k, ids: (i, 0))
    operands = [x, fronts]
    in_specs = [
        pl.BlockSpec((count, width, lanes), lambda i, k, ids: (0, 0, 0)),
        pl.BlockSpec((1, 2, tile, width), front_block),
    ]
    if not first:
        operands.append(acc)
        in_specs.append(acc_spec)
    aliases = {}
    scratch = []
    if last:
        operands += [rhs, s]
        in_specs += [row_spec, row_spec]
        aliases = {len(operands): 0}
        out_shape = [
            jax.ShapeDtypeStruct((rows, lanes), jnp.float32),
            jax.ShapeDtypeStruct((rows, lanes), jnp.bfloat16),
        ]
        out_specs = [row_spec, row_spec]
        scratch = [pltpu.VMEM((2, tile, lanes), jnp.float32)]
    else:
        out_shape = jax.ShapeDtypeStruct((2, rows, lanes), jnp.float32)
        out_specs = acc_spec
    flops = 4 * rows * width * count * lanes
    return pl.pallas_call(
        functools.partial(mul_kernel, first, last),
        grid_spec=pltpu.PrefetchScalarGridSpec(
            num_scalar_prefetch=1,
            grid=(rows // tile, count),
            in_specs=in_specs,
            out_specs=out_specs,
            scratch_shapes=scratch,
        ),
        out_shape=out_shape,
        input_output_aliases=aliases,
        compiler_params=pltpu.CompilerParams(vmem_limit_bytes=24 * 1024 * 1024),
        cost_estimate=pl.CostEstimate(
            flops=flops, bytes_accessed=4 * rows * width * count, transcendentals=0
        ),
    )(ids, *operands)


def local(rhs, fronts, wave_sq, pml_width):
    _, rhs_count, row_count, components, columns = rhs.shape
    panels = lax.axis_size("panel")
    front = lax.axis_size("front")
    panel = lax.axis_index("panel")
    place = lax.axis_index("front").astype(jnp.int32)
    rows = row_count * columns
    lanes = components * rhs_count
    masks = [1 << b for b in reversed(range(front.bit_length() - 1))]

    def exchange(values, mask, source, target):
        pairs = [(source * front + (j ^ mask), target * front + j) for j in range(front)]
        return lax.ppermute(values, ("panel", "front"), pairs)

    def shift_panel(values, by):
        pairs = [
            (p * front + j, (p + by) * front + j)
            for p in range(panels)
            for j in range(front)
            if 0 <= p + by < panels
        ]
        return lax.ppermute(values, ("panel", "front"), pairs)

    def chunk_ids(active, offsets):
        return jnp.stack([active] + [place ^ o for o in offsets]).astype(jnp.int32)

    rhs_t = rhs[0].transpose(1, 3, 2, 0).reshape(rows, lanes)
    rhs_next = shift_panel(rhs_t, -1)
    own = rhs_t.astype(jnp.bfloat16)[None]
    s = rhs_t
    for q in range(panels):
        active = (panel == q).astype(jnp.int32)
        there = exchange(own, masks[0], max(q - 1, 0), q)
        here = own if q == 0 else exchange(own, 0, q - 1, q)
        held = jnp.concatenate([here, there])
        offsets = [0, masks[0]]
        fresh, fresh_offsets = held, offsets
        acc = None
        for mask in masks[1:-2]:
            more = exchange(held, mask, q, q)
            acc = multiply(chunk_ids(active, fresh_offsets), fresh, fronts, acc)
            fresh, fresh_offsets = more, [o ^ mask for o in offsets]
            held = jnp.concatenate([held, more])
            offsets = offsets + fresh_offsets
        mask, end = masks[-2:]
        third = exchange(held, mask, q, q)
        beside_held = exchange(held, end, q, q)
        acc = multiply(chunk_ids(active, fresh_offsets), fresh, fronts, acc)
        beside_third = exchange(third, end, q, q)
        third_offsets = [o ^ mask for o in offsets]
        acc = multiply(
            chunk_ids(active, third_offsets + [o ^ end for o in offsets]),
            jnp.concatenate([third, beside_held]),
            fronts,
            acc,
        )
        s, own = multiply(
            chunk_ids(active, [o ^ end for o in third_offsets]),
            beside_third,
            fronts,
            acc,
            rhs_next,
            s,
        )
        own = own[None]

    cells = s.reshape(row_count, columns, lanes)
    narrow = cells.astype(jnp.bfloat16)
    before = shift_panel(narrow, 1).astype(jnp.float32)
    after = shift_panel(narrow, -1).astype(jnp.float32)
    above = lax.ppermute(narrow[-1:], "front", [(j, j + 1) for j in range(front - 1)])
    below = lax.ppermute(narrow[:1], "front", [(j + 1, j) for j in range(front - 1)])
    tall = jnp.concatenate([above.astype(jnp.float32), cells, below.astype(jnp.float32)])
    beside = before + after + tall[2:] + tall[:-2]
    wide = jnp.pad(cells, ((0, 0), (1, 1), (0, 0)))
    beside = beside + wide[:, 2:] + wide[:, :-2]
    plane_rows = place * row_count + jnp.arange(row_count, dtype=jnp.int32)
    row_pos = plane_rows.astype(jnp.float32)
    total_rows = row_count * front
    thick = pml_width.astype(jnp.float32)
    absorb = (
        2.0
        * (jnp.maximum(0.0, thick - row_pos) + jnp.maximum(0.0, row_pos - (total_rows - 1 - thick)))
        / thick
    )
    turned = jnp.concatenate([-cells[:, :, rhs_count:], cells[:, :, :rhs_count]], axis=2)
    applied = (6.0 - wave_sq[0])[:, :, None] * cells + absorb[:, None, None] * turned - beside
    residual = rhs_t.reshape(cells.shape) - applied

    def back(values):
        values = values.reshape(row_count, columns, components, rhs_count)
        return values.transpose(3, 0, 2, 1)[None]

    return (back(cells), back(residual))


def solution(mesh):
    return jax.shard_map(
        local,
        mesh=mesh,
        in_specs=(
            P("panel", None, "front", None, None),
            P("panel", None, "front", None),
            P("panel", "front", None),
            P("panel"),
        ),
        out_specs=(P("panel", None, "front", None, None), P("panel", None, "front", None, None)),
        check_vma=False,
    )
```

time: 462 us -> 216 us (0.47)
  matrix products: 154 us -> 0 us
  waiting for transfers between devices: 245 us -> 92.4 us
  Pallas kernels: 0 us -> 47.8 us
  starting transfers between devices: 20.5 us -> 64.4 us
  other arithmetic: 15.1 us -> 1.54 us
  between operations: 14.5 us -> 1.94 us
    all_gather x4 -> x0, waiting for transfers between devices: 204 us -> none  [apply_front(): vector_piece = lax.all_gather(combined, 'front', axis=1, tiled=True)]
    dot_general x16 -> x0, matrix products: 154 us -> none  [the longest x4 39.9 us: apply_front(): lax.dot_general(part_re, front_im, dims, preferred_element_type=jnp.float32)]
    ppermute x8 -> x24, waiting for transfers between devices: 40.2 us -> 92.4 us  [the longest x19 88.4 us: exchange(): return lax.ppermute(values, ('panel', 'front'), pairs)]
    pallas_call x0 -> x12, Pallas kernels: none -> 47.8 us  [multiply(): pl.pallas_call(functools.partial(mul_kernel, first, last), grid_spec=pltp...]
    ppermute x8 -> x24, starting transfers between devices: 20.5 us -> 64.4 us  [the longest x3 33.2 us: shift_panel(): return lax.ppermute(values, ('panel', 'front'), pairs)]
    convert_element_type x6 -> x3, other arithmetic: 9.6 us -> 0.05 us  [the longest x1 0.04 us: local(): narrow = cells.astype(jnp.bfloat16)]
    slice x4 -> x1, local copies, waits for them, and re-layouts: 6.84 us -> 0.01 us  [local(): narrow[:1]]
  transfers between devices with their start and end apart: 12 -> 24, of which waited for: 12 -> 5; matrix products, arithmetic and copies ran while one was open for 0% -> 2% of each run, Pallas kernels for 0% -> 15%
where the time goes in v1:
time: 216 us; the launch traced here: 215 us
  waiting for transfers between devices  92.4 us (43%)
  starting transfers between devices  64.4 us (30%)
  Pallas kernels  47.8 us (22%)
  local copies, waits for them, and re-layouts  6.87 us (3%)
    ppermute x19, waiting for transfers between devices, exchange(): return lax.ppermute(values, ('panel', 'front'), pairs)  88.4 us
    pallas_call x12, Pallas kernels, multiply(): pl.pallas_call(functools.partial(mul_kernel, first, last), grid_spec=pltp...  47.8 us
    ppermute x3, starting transfers between devices, shift_panel(): return lax.ppermute(values, ('panel', 'front'), pairs)  33.2 us
    ppermute x19, starting transfers between devices, exchange(): return lax.ppermute(values, ('panel', 'front'), pairs)  24.7 us
    ppermute x1, starting transfers between devices, local(): lax.ppermute(narrow[:1], 'front', [(j + 1, j) for j in range(front - 1)])  4.6 us
  transfers between devices with their start and end apart: 24, of which 5 were waited for; matrix products, arithmetic and copies ran while one was open for 2% of the time, Pallas kernels for 15%

profile of v1, /device:TPU:10, one launch (start us, length us, event | category | flops | bytes accessed | tf_op | source)
XLA Modules:
  0.0 215.0 jit_solution(6654576400350390398)
XLA Ops:
  0.6 1.2 copy.38
  4.7 1.1 copy.32
  6.1 1.9 collective-permute-start.4
  9.0 2.4 %shard_map.59.refs_0_ = f32[2,1024,128]{2,1,0:T(8,128)S(1)} custom-call(s32[3]{0:T(128)S(1)} %add_add_fusion.4.ids_ref, bf16[2,1024,128]{2,1,0:T(8,128)(2,1)S(1)} %constant_dynamic-update-slice_fusion.x_ref, bf16[1,2,1024,8192]{3,2,1,0:T(8,128)(2,1)} %c_ref.23), custom_call_target="tpu_custom_call" | custom-call | flops 1073741824 | bytes 8388608 | tf_op jit(solution)/shard_map/pallas_call | solution.py:92
  11.4 2.5 %shard_map.60.refs_0_ = f32[2,1024,128]{2,1,0:T(8,128)S(1)} custom-call(s32[5]{0:T(128)S(1)} %stack.134.ids_ref, bf16[4,1024,128]{2,1,0:T(8,128)(2,1)S(1)} %pad_maximum_fusion.x_ref, bf16[1,2,1024,8192]{3,2,1,0:T(8,128)(2,1)} %c_ref.23, f32[2,1024,128]{2,1,0:T(8,128)S(1)} %shard_map.59.refs_0_), custom_call_target="tpu_custom_call" | custom-call | flops 2147483648 | bytes 16777216 | tf_op jit(solution)/shard_map/pallas_call | solution.py:92
  14.7 2.5 %shard_map.61 = (f32[1024,128]{1,0:T(8,128)S(1)}, bf16[1024,128]{1,0:T(8,128)(2,1)S(1)}) custom-call(s32[3]{0:T(128)S(1)} %add_add_fusion.3.ids_ref, bf16[2,1024,128]{2,1,0:T(8,128)(2,1)S(1)} %collective-permute-done.2.x_ref, bf16[1,2,1024,8192]{3,2,1,0:T(8,128)(2,1)} %c_ref.23, ...), custom_call_target="tpu_custom_call", output_to_operand_aliasing={{0}: (5, {})} | custom-call | flops 1073741824 | bytes 8388608 | tf_op jit(solution)/shard_map/pallas_call | solution.py:92
  21.0 2.4 %shard_map.62.refs_0_ = f32[2,1024,128]{2,1,0:T(8,128)S(1)} custom-call(s32[3]{0:T(128)S(1)} %add_add_fusion.5.ids_ref, bf16[2,1024,128]{2,1,0:T(8,128)(2,1)S(1)} %constant_dynamic-update-slice_fusion.2.x_ref, bf16[1,2,1024,8192]{3,2,1,0:T(8,128)(2,1)} %c_ref.23), custom_call_target="tpu_custom_call" | custom-call | flops 1073741824 | bytes 8388608 | tf_op jit(solution)/shard_map/pallas_call | solution.py:92
  23.5 2.5 %shard_map.63.refs_0_ = f32[2,1024,128]{2,1,0:T(8,128)S(1)} custom-call(s32[5]{0:T(128)S(1)} %stack.138.ids_ref, bf16[4,1024,128]{2,1,0:T(8,128)(2,1)S(1)} %pad_maximum_fusion.1.x_ref, bf16[1,2,1024,8192]{3,2,1,0:T(8,128)(2,1)} %c_ref.23, f32[2,1024,128]{2,1,0:T(8,128)S(1)} %shard_map.62.refs_0_), custom_call_target="tpu_custom_call" | custom-call | flops 2147483648 | bytes 16777216 | tf_op jit(solution)/shard_map/pallas_call | solution.py:92
  26.0 2.5 %shard_map.64 = (f32[1024,128]{1,0:T(8,128)S(1)}, bf16[1024,128]{1,0:T(8,128)(2,1)S(1)}) custom-call(s32[3]{0:T(128)S(1)} %add_add_fusion.2.ids_ref, bf16[2,1024,128]{2,1,0:T(8,128)(2,1)S(1)} %collective-permute-done.8.x_ref, bf16[1,2,1024,8192]{3,2,1,0:T(8,128)(2,1)} %c_ref.23, ...), custom_call_target="tpu_custom_call", output_to_operand_aliasing={{0}: (5, {})} | custom-call | flops 1073741824 | bytes 8388608 | tf_op jit(solution)/shard_map/pallas_call | solution.py:92
  28.5 1.3 collective-permute-start.10
  29.8 1.3 collective-permute-start.11
  31.1 78.2 %collective-permute-done.10 = bf16[1,1024,128]{2,1,0:T(8,128)(2,1)S(1)} collective-permute-done((bf16[1,1024,128]{2,1,0:T(8,128)(2,1)S(1)}, bf16[1,1024,128]{2,1,0:T(8,128)(2,1)S(1)}, u32[]{:S(2)}, u32[]{:S(2)}) %collective-permute-start.10) | collective-permute-done | bytes 262176 | tf_op jit(solution)/shard_map/ppermute | solution.py:122
  109.4 4.2 %collective-permute-start.12 = (bf16[2,1024,128]{2,1,0:T(8,128)(2,1)S(1)}, bf16[2,1024,128]{2,1,0:T(8,128)(2,1)S(1)}, u32[]{:S(2)}, u32[]{:S(2)}) collective-permute-start(bf16[2,1024,128]{2,1,0:T(8,128)(2,1)S(1)} %constant_dynamic-update-slice_fusion.4.x_ref), channel_id=1, source_target_pairs={{18,16},{19,17},{16,18},{17,19},{22,20},{23,21},{20,22},{21,23}} | collective-permute-start | bytes 1572872 | tf_op jit(solution)/shard_map/ppermute | solution.py:122
  113.6 3.4 %collective-permute-start.14 = (bf16[2,1024,128]{2,1,0:T(8,128)(2,1)S(1)}, bf16[2,1024,128]{2,1,0:T(8,128)(2,1)S(1)}, u32[]{:S(2)}, u32[]{:S(2)}) collective-permute-start(bf16[2,1024,128]{2,1,0:T(8,128)(2,1)S(1)} %constant_dynamic-update-slice_fusion.4.x_ref), channel_id=1, source_target_pairs={{17,16},{16,17},{19,18},{18,19},{21,20},{20,21},{23,22},{22,23}} | collective-permute-start | bytes 1572872 | tf_op jit(solution)/shard_map/ppermute | solution.py:122
  117.2 3.5 %collective-permute-done.12 = bf16[2,1024,128]{2,1,0:T(8,128)(2,1)S(1)} collective-permute-done((bf16[2,1024,128]{2,1,0:T(8,128)(2,1)S(1)}, bf16[2,1024,128]{2,1,0:T(8,128)(2,1)S(1)}, u32[]{:S(2)}, u32[]{:S(2)}) %collective-permute-start.12) | collective-permute-done | bytes 524320 | tf_op jit(solution)/shard_map/ppermute | solution.py:122
  120.7 3.4 %collective-permute-start.13 = (bf16[2,1024,128]{2,1,0:T(8,128)(2,1)S(1)}, bf16[2,1024,128]{2,1,0:T(8,128)(2,1)S(1)}, u32[]{:S(2)}, u32[]{:S(2)}) collective-permute-start(bf16[2,1024,128]{2,1,0:T(8,128)(2,1)S(1)} %collective-permute-done.12), channel_id=1, source_target_pairs={{17,16},{16,17},{19,18},{18,19},{21,20},{20,21},{23,22},{22,23}} | collective-permute-start | bytes 1572872 | tf_op jit(solution)/shard_map/ppermute | solution.py:122
  124.2 6.3 %shard_map.65.refs_0_ = f32[2,1024,128]{2,1,0:T(8,128)S(1)} custom-call(s32[3]{0:T(128)S(1)} %add_add_fusion.6.ids_ref, bf16[2,1024,128]{2,1,0:T(8,128)(2,1)S(1)} %constant_dynamic-update-slice_fusion.4.x_ref, bf16[1,2,1024,8192]{3,2,1,0:T(8,128)(2,1)} %c_ref.23), custom_call_target="tpu_custom_call" | custom-call | flops 1073741824 | bytes 8388608 | tf_op jit(solution)/shard_map/pallas_call | solution.py:92
  130.7 11.5 %shard_map.66.refs_0_ = f32[2,1024,128]{2,1,0:T(8,128)S(1)} custom-call(s32[5]{0:T(128)S(1)} %stack.140.ids_ref, bf16[4,1024,128]{2,1,0:T(8,128)(2,1)S(1)} %pad_maximum_fusion.2.x_ref, bf16[1,2,1024,8192]{3,2,1,0:T(8,128)(2,1)} %c_ref.23, f32[2,1024,128]{2,1,0:T(8,128)S(1)} %shard_map.65.refs_0_), custom_call_target="tpu_custom_call" | custom-call | flops 2147483648 | bytes 16777216 | tf_op jit(solution)/shard_map/pallas_call | solution.py:92
  142.2 6.8 %shard_map.67 = (f32[1024,128]{1,0:T(8,128)S(1)}, bf16[1024,128]{1,0:T(8,128)(2,1)S(1)}) custom-call(s32[3]{0:T(128)S(1)} %add_add_fusion.1.ids_ref, bf16[2,1024,128]{2,1,0:T(8,128)(2,1)S(1)} %collective-permute-done.13.x_ref, bf16[1,2,1024,8192]{3,2,1,0:T(8,128)(2,1)} %c_ref.23, ...), custom_call_target="tpu_custom_call", output_to_operand_aliasing={{0}: (5, {})} | custom-call | flops 1073741824 | bytes 8388608 | tf_op jit(solution)/shard_map/pallas_call | solution.py:92
  149.0 1.3 collective-permute-start.15
  150.3 1.3 collective-permute-start.16
  151.6 6.6 %collective-permute-done.16 = bf16[1,1024,128]{2,1,0:T(8,128)(2,1)S(1)} collective-permute-done((bf16[1,1024,128]{2,1,0:T(8,128)(2,1)S(1)}, bf16[1,1024,128]{2,1,0:T(8,128)(2,1)S(1)}, u32[]{:S(2)}, u32[]{:S(2)}) %collective-permute-start.16) | collective-permute-done | bytes 262176 | tf_op jit(solution)/shard_map/ppermute | solution.py:122
  161.7 2.4 %shard_map.68.refs_0_ = f32[2,1024,128]{2,1,0:T(8,128)S(1)} custom-call(s32[3]{0:T(128)S(1)} %add_add_fusion.7.ids_ref, bf16[2,1024,128]{2,1,0:T(8,128)(2,1)S(1)} %constant_dynamic-update-slice_fusion.6.x_ref, bf16[1,2,1024,8192]{3,2,1,0:T(8,128)(2,1)} %c_ref.23), custom_call_target="tpu_custom_call" | custom-call | flops 1073741824 | bytes 8388608 | tf_op jit(solution)/shard_map/pallas_call | solution.py:92
  164.2 2.5 %shard_map.69.refs_0_ = f32[2,1024,128]{2,1,0:T(8,128)S(1)} custom-call(s32[5]{0:T(128)S(1)} %stack.142.ids_ref, bf16[4,1024,128]{2,1,0:T(8,128)(2,1)S(1)} %pad_maximum_fusion.3.x_ref, bf16[1,2,1024,8192]{3,2,1,0:T(8,128)(2,1)} %c_ref.23, f32[2,1024,128]{2,1,0:T(8,128)S(1)} %shard_map.68.refs_0_), custom_call_target="tpu_custom_call" | custom-call | flops 2147483648 | bytes 16777216 | tf_op jit(solution)/shard_map/pallas_call | solution.py:92
  166.7 3.7 %shard_map.70 = (f32[1024,128]{1,0:T(8,128)S(1)}, bf16[1024,128]{1,0:T(8,128)(2,1)}) custom-call(s32[3]{0:T(128)S(1)} %add_add_fusion.ids_ref, bf16[2,1024,128]{2,1,0:T(8,128)(2,1)S(1)} %collective-permute-done.18.x_ref, bf16[1,2,1024,8192]{3,2,1,0:T(8,128)(2,1)} %c_ref.23, f32[2,1024,128]{2,1,0:T(8,128)S(1)} %shard_map.69.refs_0_, ...), custom_call_target="tpu_custom_call", output_to_operand_aliasing={{0}: (5, {})} | custom-call | flops 1073741824 | bytes 8388608 | tf_op jit(solution)/shard_map/pallas_call | solution.py:92
  170.6 29.4 %collective-permute-start.20 = (bf16[8,128,128]{1,2,0:T(8,128)(2,1)S(1)}, bf16[8,128,128]{1,2,0:T(8,128)(2,1)S(1)}, u32[]{:S(2)}, u32[]{:S(2)}) collective-permute-start(bf16[8,128,128]{1,2,0:T(8,128)(2,1)S(1)} %convert_element_type.48), channel_id=1, source_target_pairs={{0,8},{1,9},{2,10},{3,11},{4,12},{5,13},{6,14},{7,15},{8,16},{9,17... | collective-permute-start | bytes 786440 | tf_op jit(solution)/shard_map/ppermute | solution.py:131
  200.0 1.9 collective-permute-start.21
  202.0 4.6 %collective-permute-start.22 = (bf16[1,128,128]{1,2,0:T(8,128)(2,1)S(1)}, bf16[1,128,128]{1,2,0:T(8,128)(2,1)S(1)}, u32[]{:S(2)}, u32[]{:S(2)}) collective-permute-start(bf16[1,128,128]{1,2,0:T(8,128)(2,1)S(1)} %get-tuple-element.20), channel_id=1, source_target_pairs={{1,0},{2,1},{3,2},{4,3},{5,4},{6,5},{7,6},{9,8},{10,9},{11,10},{12... | collective-permute-start | bytes 98312 | tf_op jit(solution)/shard_map/ppermute | solution.py:181
  206.6 1.9 collective-permute-start.23
  208.9 1.2 copy.28
  210.1 3.2 %collective-permute-done.23 = bf16[1,128,128]{1,2,0:T(8,128)(2,1)S(1)} collective-permute-done((bf16[1,128,128]{1,2,0:T(8,128)(2,1)S(1)}, bf16[1,128,128]{1,2,0:T(8,128)(2,1)S(1)}, u32[]{:S(2)}, u32[]{:S(2)}) %collective-permute-start.23) | collective-permute-done | bytes 32800 | tf_op jit(solution)/shard_map/ppermute | solution.py:180
  213.8 1.2 copy.29
  (76 shorter events, 12.9 us)
Async XLA Ops:
  2.5 0.7 collective-permute-start
  3.3 4.9 %collective-permute-start.1 = (bf16[2,1024,128]{2,1,0:T(8,128)(2,1)S(1)}, bf16[2,1024,128]{2,1,0:T(8,128)(2,1)S(1)}, u32[]{:S(2)}, u32[]{:S(2)}) collective-permute-start(bf16[2,1024,128]{2,1,0:T(8,128)(2,1)S(1)} %constant_dynamic-update-slice_fusion.x_ref), channel_id=1, source_target_pairs={{2,0},{3,1},{0,2},{1,3},{6,4},{7,5},{4,6},{5,7}} | collective-permute-start | bytes 1572872 | tf_op jit(solution)/shard_map/ppermute | solution.py:122
  4.0 7.3 %collective-permute-start.3 = (bf16[2,1024,128]{2,1,0:T(8,128)(2,1)S(1)}, bf16[2,1024,128]{2,1,0:T(8,128)(2,1)S(1)}, u32[]{:S(2)}, u32[]{:S(2)}) collective-permute-start(bf16[2,1024,128]{2,1,0:T(8,128)(2,1)S(1)} %constant_dynamic-update-slice_fusion.x_ref), channel_id=1, source_target_pairs={{1,0},{0,1},{3,2},{2,3},{5,4},{4,5},{7,6},{6,7}} | collective-permute-start | bytes 1572872 | tf_op jit(solution)/shard_map/ppermute | solution.py:122
  6.1 8.6 %collective-permute-start.4 = (f32[1024,128]{1,0:T(8,128)S(1)}, f32[1024,128]{1,0:T(8,128)S(1)}, u32[]{:S(2)}, u32[]{:S(2)}) collective-permute-start(f32[1024,128]{1,0:T(8,128)S(1)} %copy.18.refs_2_), channel_id=1, source_target_pairs={{8,0},{9,1},{10,2},{11,3},{12,4},{13,5},{14,6},{15,7},{16,8},{17,9... | collective-permute-start | bytes 1572872 | tf_op jit(solution)/shard_map/ppermute | solution.py:131
  8.2 6.5 %collective-permute-start.2 = (bf16[2,1024,128]{2,1,0:T(8,128)(2,1)S(1)}, bf16[2,1024,128]{2,1,0:T(8,128)(2,1)S(1)}, u32[]{:S(2)}, u32[]{:S(2)}) collective-permute-start(bf16[2,1024,128]{2,1,0:T(8,128)(2,1)S(1)} %collective-permute-done.1), channel_id=1, source_target_pairs={{1,0},{0,1},{3,2},{2,3},{5,4},{4,5},{7,6},{6,7}} | collective-permute-start | bytes 1572872 | tf_op jit(solution)/shard_map/ppermute | solution.py:122
  17.2 1.4 collective-permute-start.5
  17.9 0.7 collective-permute-start.6
  18.6 1.6 collective-permute-start.7
  19.3 4.0 %collective-permute-start.9 = (bf16[2,1024,128]{2,1,0:T(8,128)(2,1)S(1)}, bf16[2,1024,128]{2,1,0:T(8,128)(2,1)S(1)}, u32[]{:S(2)}, u32[]{:S(2)}) collective-permute-start(bf16[2,1024,128]{2,1,0:T(8,128)(2,1)S(1)} %constant_dynamic-update-slice_fusion.2.x_ref), channel_id=1, source_target_pairs={{9,8},{8,9},{11,10},{10,11},{13,12},{12,13},{15,14},{14,15}} | collective-permute-start | bytes 1572872 | tf_op jit(solution)/shard_map/ppermute | solution.py:122
  20.2 5.8 %collective-permute-start.8 = (bf16[2,1024,128]{2,1,0:T(8,128)(2,1)S(1)}, bf16[2,1024,128]{2,1,0:T(8,128)(2,1)S(1)}, u32[]{:S(2)}, u32[]{:S(2)}) collective-permute-start(bf16[2,1024,128]{2,1,0:T(8,128)(2,1)S(1)} %collective-permute-done.7), channel_id=1, source_target_pairs={{9,8},{8,9},{11,10},{10,11},{13,12},{12,13},{15,14},{14,15}} | collective-permute-start | bytes 1572872 | tf_op jit(solution)/shard_map/ppermute | solution.py:122
  28.5 80.8 %collective-permute-start.10 = (bf16[1,1024,128]{2,1,0:T(8,128)(2,1)S(1)}, bf16[1,1024,128]{2,1,0:T(8,128)(2,1)S(1)}, u32[]{:S(2)}, u32[]{:S(2)}) collective-permute-start(bf16[1,1024,128]{2,1,0:T(8,128)(2,1)S(1)} %bitcast.52), channel_id=1, source_target_pairs={{8,16},{9,17},{10,18},{11,19},{12,20},{13,21},{14,22},{15,23}} | collective-permute-start | bytes 786440 | tf_op jit(solution)/shard_map/ppermute | solution.py:122
  29.8 79.5 %collective-permute-start.11 = (bf16[1,1024,128]{2,1,0:T(8,128)(2,1)S(1)}, bf16[1,1024,128]{2,1,0:T(8,128)(2,1)S(1)}, u32[]{:S(2)}, u32[]{:S(2)}) collective-permute-start(bf16[1,1024,128]{2,1,0:T(8,128)(2,1)S(1)} %bitcast.53), channel_id=1, source_target_pairs={{12,16},{13,17},{14,18},{15,19},{8,20},{9,21},{10,22},{11,23}} | collective-permute-start | bytes 786440 | tf_op jit(solution)/shard_map/ppermute | solution.py:122
  109.4 11.3 %collective-permute-start.12 = (bf16[2,1024,128]{2,1,0:T(8,128)(2,1)S(1)}, bf16[2,1024,128]{2,1,0:T(8,128)(2,1)S(1)}, u32[]{:S(2)}, u32[]{:S(2)}) collective-permute-start(bf16[2,1024,128]{2,1,0:T(8,128)(2,1)S(1)} %constant_dynamic-update-slice_fusion.4.x_ref), channel_id=1, source_target_pairs={{18,16},{19,17},{16,18},{17,19},{22,20},{23,21},{20,22},{21,23}} | collective-permute-start | bytes 1572872 | tf_op jit(solution)/shard_map/ppermute | solution.py:122
  113.6 17.0 %collective-permute-start.14 = (bf16[2,1024,128]{2,1,0:T(8,128)(2,1)S(1)}, bf16[2,1024,128]{2,1,0:T(8,128)(2,1)S(1)}, u32[]{:S(2)}, u32[]{:S(2)}) collective-permute-start(bf16[2,1024,128]{2,1,0:T(8,128)(2,1)S(1)} %constant_dynamic-update-slice_fusion.4.x_ref), channel_id=1, source_target_pairs={{17,16},{16,17},{19,18},{18,19},{21,20},{20,21},{23,22},{22,23}} | collective-permute-start | bytes 1572872 | tf_op jit(solution)/shard_map/ppermute | solution.py:122
  120.7 21.5 %collective-permute-start.13 = (bf16[2,1024,128]{2,1,0:T(8,128)(2,1)S(1)}, bf16[2,1024,128]{2,1,0:T(8,128)(2,1)S(1)}, u32[]{:S(2)}, u32[]{:S(2)}) collective-permute-start(bf16[2,1024,128]{2,1,0:T(8,128)(2,1)S(1)} %collective-permute-done.12), channel_id=1, source_target_pairs={{17,16},{16,17},{19,18},{18,19},{21,20},{20,21},{23,22},{22,23}} | collective-permute-start | bytes 1572872 | tf_op jit(solution)/shard_map/ppermute | solution.py:122
  130.7 28.3 %copy-start = (f32[1,64,8,2,128]{4,3,2,1,0:T(2,128)S(1)}, f32[1,64,8,2,128]{4,3,2,1,0:T(2,128)}, u32[]{:S(2)}) copy-start(f32[1,64,8,2,128]{4,3,2,1,0:T(2,128)} %param.4) | copy-start | bytes 1572868
  130.7 30.1 %copy-start.1 = (f32[1,8,128]{2,1,0:T(8,128)S(1)}, f32[1,8,128]{2,1,0:T(8,128)}, u32[]{:S(2)}) copy-start(f32[1,8,128]{2,1,0:T(8,128)} %param.6) | copy-start | bytes 12292
  149.0 2.6 %collective-permute-start.15 = (bf16[1,1024,128]{2,1,0:T(8,128)(2,1)S(1)}, bf16[1,1024,128]{2,1,0:T(8,128)(2,1)S(1)}, u32[]{:S(2)}, u32[]{:S(2)}) collective-permute-start(bf16[1,1024,128]{2,1,0:T(8,128)(2,1)S(1)} %bitcast.54), channel_id=1, source_target_pairs={{16,24},{17,25},{18,26},{19,27},{20,28},{21,29},{22,30},{23,31}} | collective-permute-start | bytes 786440 | tf_op jit(solution)/shard_map/ppermute | solution.py:122
  150.3 8.0 %collective-permute-start.16 = (bf16[1,1024,128]{2,1,0:T(8,128)(2,1)S(1)}, bf16[1,1024,128]{2,1,0:T(8,128)(2,1)S(1)}, u32[]{:S(2)}, u32[]{:S(2)}) collective-permute-start(bf16[1,1024,128]{2,1,0:T(8,128)(2,1)S(1)} %bitcast.55), channel_id=1, source_target_pairs={{20,24},{21,25},{22,26},{23,27},{16,28},{17,29},{18,30},{19,31}} | collective-permute-start | bytes 786440 | tf_op jit(solution)/shard_map/ppermute | solution.py:122
  158.3 2.5 %collective-permute-start.17 = (bf16[2,1024,128]{2,1,0:T(8,128)(2,1)S(1)}, bf16[2,1024,128]{2,1,0:T(8,128)(2,1)S(1)}, u32[]{:S(2)}, u32[]{:S(2)}) collective-permute-start(bf16[2,1024,128]{2,1,0:T(8,128)(2,1)S(1)} %constant_dynamic-update-slice_fusion.6.x_ref), channel_id=1, source_target_pairs={{26,24},{27,25},{24,26},{25,27},{30,28},{31,29},{28,30},{29,31}} | collective-permute-start | bytes 1572872 | tf_op jit(solution)/shard_map/ppermute | solution.py:122
  160.0 4.0 %collective-permute-start.19 = (bf16[2,1024,128]{2,1,0:T(8,128)(2,1)S(1)}, bf16[2,1024,128]{2,1,0:T(8,128)(2,1)S(1)}, u32[]{:S(2)}, u32[]{:S(2)}) collective-permute-start(bf16[2,1024,128]{2,1,0:T(8,128)(2,1)S(1)} %constant_dynamic-update-slice_fusion.6.x_ref), channel_id=1, source_target_pairs={{25,24},{24,25},{27,26},{26,27},{29,28},{28,29},{31,30},{30,31}} | collective-permute-start | bytes 1572872 | tf_op jit(solution)/shard_map/ppermute | solution.py:122
  160.8 5.9 %collective-permute-start.18 = (bf16[2,1024,128]{2,1,0:T(8,128)(2,1)S(1)}, bf16[2,1024,128]{2,1,0:T(8,128)(2,1)S(1)}, u32[]{:S(2)}, u32[]{:S(2)}) collective-permute-start(bf16[2,1024,128]{2,1,0:T(8,128)(2,1)S(1)} %collective-permute-done.17), channel_id=1, source_target_pairs={{25,24},{24,25},{27,26},{26,27},{29,28},{28,29},{31,30},{30,31}} | collective-permute-start | bytes 1572872 | tf_op jit(solution)/shard_map/ppermute | solution.py:122
  170.6 42.7 %collective-permute-start.20 = (bf16[8,128,128]{1,2,0:T(8,128)(2,1)S(1)}, bf16[8,128,128]{1,2,0:T(8,128)(2,1)S(1)}, u32[]{:S(2)}, u32[]{:S(2)}) collective-permute-start(bf16[8,128,128]{1,2,0:T(8,128)(2,1)S(1)} %convert_element_type.48), channel_id=1, source_target_pairs={{0,8},{1,9},{2,10},{3,11},{4,12},{5,13},{6,14},{7,15},{8,16},{9,17... | collective-permute-start | bytes 786440 | tf_op jit(solution)/shard_map/ppermute | solution.py:131
  200.0 13.3 %collective-permute-start.21 = (bf16[8,128,128]{1,2,0:T(8,128)(2,1)S(1)}, bf16[8,128,128]{1,2,0:T(8,128)(2,1)S(1)}, u32[]{:S(2)}, u32[]{:S(2)}) collective-permute-start(bf16[8,128,128]{1,2,0:T(8,128)(2,1)S(1)} %convert_element_type.48), channel_id=1, source_target_pairs={{8,0},{9,1},{10,2},{11,3},{12,4},{13,5},{14,6},{15,7},{16,8},{17,9... | collective-permute-start | bytes 786440 | tf_op jit(solution)/shard_map/ppermute | solution.py:131
  202.0 8.1 %collective-permute-start.22 = (bf16[1,128,128]{1,2,0:T(8,128)(2,1)S(1)}, bf16[1,128,128]{1,2,0:T(8,128)(2,1)S(1)}, u32[]{:S(2)}, u32[]{:S(2)}) collective-permute-start(bf16[1,128,128]{1,2,0:T(8,128)(2,1)S(1)} %get-tuple-element.20), channel_id=1, source_target_pairs={{1,0},{2,1},{3,2},{4,3},{5,4},{6,5},{7,6},{9,8},{10,9},{11,10},{12... | collective-permute-start | bytes 98312 | tf_op jit(solution)/shard_map/ppermute | solution.py:181
  206.6 6.7 %collective-permute-start.23 = (bf16[1,128,128]{1,2,0:T(8,128)(2,1)S(1)}, bf16[1,128,128]{1,2,0:T(8,128)(2,1)S(1)}, u32[]{:S(2)}, u32[]{:S(2)}) collective-permute-start(bf16[1,128,128]{1,2,0:T(8,128)(2,1)S(1)} %get-tuple-element.21), channel_id=1, source_target_pairs={{0,1},{1,2},{2,3},{3,4},{4,5},{5,6},{6,7},{8,9},{9,10},{10,11},{11... | collective-permute-start | bytes 98312 | tf_op jit(solution)/shard_map/ppermute | solution.py:180
